TPU v7x, 32 devices: a whole 2x2x4 slice. The times are simulated.
32 devices in a mesh: groups: 2 (over y), dp: 4 (over z), tensor: 2 (over x), sub: 2 (over core).
Axes of the slice: x: 2, y: 2, z: 4, core: 2. Of those that a mesh axis runs over, the one named last changes fastest.
Arguments:
- activations: bfloat16 [4096, 8192], P(('groups', 'dp'), ('tensor', 'sub')), parts along dimension 0, may hold values from -6 to 6
- cotangents: bfloat16 [4096, 28672], P(('groups', 'dp'), ('tensor', 'sub')), parts along dimension 0, may hold values from -0.125 to 0.125
- block_rows: int32 [4, 256], P(('tensor', 'sub')), may hold values from 0 to 127, as said below
- block_cols: int32 [4, 256], P(('tensor', 'sub')), may hold values from 0 to 111
- live_counts: int32 [4], P(('tensor', 'sub')), may hold values from 128 to 256, as said below
- owner_device: int32 [4, 256], replicated, may hold values from 0 to 15, as said below
- owner_slot: int32 [4, 256], replicated, may hold values from 0 to 63
Outputs:
- owned_grads: float32 [32, 64, 4096], P(('groups', 'dp', 'tensor', 'sub')), parts along dimension 0
There are 2 independent parts, one for each index of `groups`. A program takes and returns all parts, laid end to end along the dimension named above; an argument that names none is the same for every part. Nothing has to cross between parts.
Inputs may be any that keep to these rules, and one draw needn't show every extreme that they name: Within one column group the pairs of block_rows and block_cols name distinct blocks. `live_counts`: some column group uses all 256 slots. `owner_device`: owner devices are numbered dp index times 4 plus column group. Each owner holds exactly 64 slots over all groups, one for each owner_slot value. Of one group's slots, exactly 64 have owners at each dp index, and these carry distinct owner_slot values. One group has at most 16 slots at one owner, and exactly 16 at some.
All inputs are finite; a program needn't handle non-finite values.
Results may differ from a plain program's by a relative error of at most 0.0003.
Values may be sent and summed in bfloat16 or wider, within the bound.
A program may use at most 128 MiB of HBM per device.

v0:
```python
import jax
import jax.numpy as jnp
from jax import lax
from jax.sharding import PartitionSpec as P

BS = 64
SLOTS = 256


def local(activations, cotangents, block_rows, block_cols, live_counts, owner_device, owner_slot):
    columns = lax.axis_size(("tensor", "sub"))
    data_size = lax.axis_size("dp")
    my_column = lax.axis_index(("tensor", "sub"))
    my_data = lax.axis_index("dp")
    tokens_here = activations.shape[0]
    gathered = lax.all_gather(activations, ("tensor", "sub"), axis=1, tiled=True)
    act_tiles = gathered.reshape(tokens_here, -1, BS)
    cot_tiles = cotangents.reshape(tokens_here, -1, BS)
    block_width = min(32, SLOTS)
    blocks = SLOTS // block_width
    per_owner = SLOTS // data_size
    position = owner_device // columns * per_owner + owner_slot
    group_ids = jnp.broadcast_to(jnp.arange(columns, dtype=jnp.int32)[:, None], position.shape)
    slot_ids = jnp.broadcast_to(jnp.arange(SLOTS, dtype=jnp.int32)[None, :], position.shape)
    inverse = jnp.zeros_like(owner_device).at[group_ids, position].set(slot_ids)
    own_inverse = lax.dynamic_index_in_dim(inverse, my_column, 0, keepdims=False)
    ordered_rows = block_rows[0][own_inverse]
    ordered_cols = block_cols[0][own_inverse]
    ordered_live = own_inverse < live_counts[0]

    def tile_block(pieces):
        row_ids, col_ids, keep_mask = pieces
        product = jnp.einsum(
            "tsa,tsb->sab",
            act_tiles[:, row_ids],
            cot_tiles[:, col_ids],
            preferred_element_type=jnp.float32,
        )
        return jnp.where(keep_mask[:, None], product.reshape(block_width, BS * BS), 0.0)

    ordered = lax.map(
        tile_block,
        (
            ordered_rows.reshape(blocks, block_width),
            ordered_cols.reshape(blocks, block_width),
            ordered_live.reshape(blocks, block_width),
        ),
    ).reshape(SLOTS, BS * BS)
    summed = lax.psum(ordered, "dp")
    own_rows = lax.dynamic_slice_in_dim(summed, my_data * per_owner, per_owner, 0)
    target_all = jnp.take_along_axis(owner_device, inverse, axis=1) % columns
    target = lax.dynamic_slice_in_dim(target_all, my_data * per_owner, per_owner, 1)
    own_target = lax.dynamic_index_in_dim(target, my_column, 0, keepdims=False)
    pair_cap = (per_owner + columns - 1) // columns
    earlier = jnp.arange(per_owner)[:, None] > jnp.arange(per_owner)[None, :]
    same_target = target[:, :, None] == target[:, None, :]
    ranking = jnp.sum(jnp.logical_and(same_target, earlier[None]), axis=2)
    ranking = jnp.minimum(ranking, pair_cap - 1)
    own_ranking = lax.dynamic_index_in_dim(ranking, my_column, 0, keepdims=False)
    outgoing = (
        jnp.zeros((columns, pair_cap, BS * BS), jnp.float32)
        .at[own_target, own_ranking]
        .set(own_rows)
    )
    incoming = lax.all_to_all(outgoing, ("tensor", "sub"), split_axis=0, concat_axis=0, tiled=True)
    fetched = incoming[jnp.arange(columns)[:, None], ranking]
    chosen = target == my_column
    return jnp.sum(jnp.where(chosen[:, :, None], fetched, 0.0), axis=0)[None]


def solution(mesh):
    placed = (
        P(("groups", "dp"), ("tensor", "sub")),
        P(("groups", "dp"), ("tensor", "sub")),
        P(("tensor", "sub"), None),
        P(("tensor", "sub"), None),
        P(("tensor", "sub")),
        P(),
        P(),
    )
    return jax.shard_map(
        local,
        mesh=mesh,
        in_specs=placed,
        out_specs=P(("groups", "dp", "tensor", "sub"), None, None),
        check_vma=False,
    )
```

profile of v0, /device:TPU:13, one launch (start us, length us, event | category | flops | bytes accessed | tf_op | source)
XLA Modules:
  0.0 379.1 jit_solution(5395705336190928699)
XLA Ops:
  6.6 4.0 %copy.12 = bf16[512,2048]{0,1:T(8,128)(2,1)} copy(bf16[512,2048]{1,0:T(8,128)(2,1)} %param.9) | data formatting | bytes 4194304 | tf_op args[0]
  10.9 4.3 %scatter_custom_fusion.1 = s32[1024]{0:T(1024)S(1)} fusion(s32[1024]{0:T(1024)S(1)} %bitcast.86, s32[1024]{0:T(1024)S(1)} %bitcast.87, s32[]{:T(128)} %constant.104.clone.1), kind=kCustom, calls=%fused_computation.58 | custom fusion | bytes 4100
  20.2 10.2 %copy.13 = bf16[512,7168]{0,1:T(8,128)(2,1)} copy(bf16[512,7168]{1,0:T(8,128)(2,1)} %param.10) | data formatting | bytes 14680064 | tf_op args[1]
  30.3 40.2 %all-gather.2.cloned.1.call-done = bf16[512,8192]{0,1:T(8,128)(2,1)} async-done(((bf16[512,2048]{0,1:T(8,128)(2,1)}), bf16[512,8192]{0,1:T(8,128)(2,1)}) %all-gather.2.cloned.1.call-update) | async-done | bytes 8388624 | tf_op jit(solution)/shard_map/all_gather | solution.py:16
  70.6 102.5 %while.10 = (s32[]{:T(128)}, f32[8,32,4096]{2,1,0:T(8,128)}, pred[8,32]{1,0:T(8,128)(4,1)S(1)}, s32[8,32]{1,0:T(8,128)S(1)}, bf16[512,128,64]{0,2,1:T(8,128)(2,1...) while((s32[]{:T(128)}, f32[8,32,4096]{2,1,0:T(8,128)}, pred[8,32]{1,0:T(8,128)(4,1)S(1)}, ...), condition=%wide.region_3.4_spmd, body=%wide.region_2.3_spmd.sunk | while | flops 134351040 | bytes 15214269 | solution.py:41
  70.6 3.8 gather_fusion
  74.4 5.4 %gather_fusion.1 = bf16[32,512,64]{1,2,0:T(8,128)(2,1)} fusion(bf16[512,128,64]{0,2,1:T(8,128)(2,1)} %get-tuple-element.128, s32[1024]{0:T(1024)S(1)} %pad_clamp_fusion.6), kind=kCustom, calls=%fused_computation.clone.1 | custom fusion | bytes 4194432 | tf_op jit(solution)/shard_map/while/body/eval_jaxpr/gather | solution.py:35
  83.4 3.8 gather_fusion
  87.2 5.4 %gather_fusion.1 = bf16[32,512,64]{1,2,0:T(8,128)(2,1)} fusion(bf16[512,128,64]{0,2,1:T(8,128)(2,1)} %get-tuple-element.128, s32[1024]{0:T(1024)S(1)} %pad_clamp_fusion.6), kind=kCustom, calls=%fused_computation.clone.1 | custom fusion | bytes 4194432 | tf_op jit(solution)/shard_map/while/body/eval_jaxpr/gather | solution.py:35
  96.2 3.8 gather_fusion
  100.0 5.4 %gather_fusion.1 = bf16[32,512,64]{1,2,0:T(8,128)(2,1)} fusion(bf16[512,128,64]{0,2,1:T(8,128)(2,1)} %get-tuple-element.128, s32[1024]{0:T(1024)S(1)} %pad_clamp_fusion.6), kind=kCustom, calls=%fused_computation.clone.1 | custom fusion | bytes 4194432 | tf_op jit(solution)/shard_map/while/body/eval_jaxpr/gather | solution.py:35
  109.0 3.8 gather_fusion
  112.8 5.4 %gather_fusion.1 = bf16[32,512,64]{1,2,0:T(8,128)(2,1)} fusion(bf16[512,128,64]{0,2,1:T(8,128)(2,1)} %get-tuple-element.128, s32[1024]{0:T(1024)S(1)} %pad_clamp_fusion.6), kind=kCustom, calls=%fused_computation.clone.1 | custom fusion | bytes 4194432 | tf_op jit(solution)/shard_map/while/body/eval_jaxpr/gather | solution.py:35
  125.6 5.4 %gather_fusion.1 = bf16[32,512,64]{1,2,0:T(8,128)(2,1)} fusion(bf16[512,128,64]{0,2,1:T(8,128)(2,1)} %get-tuple-element.128, s32[1024]{0:T(1024)S(1)} %pad_clamp_fusion.6), kind=kCustom, calls=%fused_computation.clone.1 | custom fusion | bytes 4194432 | tf_op jit(solution)/shard_map/while/body/eval_jaxpr/gather | solution.py:35
  138.4 5.4 %gather_fusion.1 = bf16[32,512,64]{1,2,0:T(8,128)(2,1)} fusion(bf16[512,128,64]{0,2,1:T(8,128)(2,1)} %get-tuple-element.128, s32[1024]{0:T(1024)S(1)} %pad_clamp_fusion.6), kind=kCustom, calls=%fused_computation.clone.1 | custom fusion | bytes 4194432 | tf_op jit(solution)/shard_map/while/body/eval_jaxpr/gather | solution.py:35
  151.2 5.4 %gather_fusion.1 = bf16[32,512,64]{1,2,0:T(8,128)(2,1)} fusion(bf16[512,128,64]{0,2,1:T(8,128)(2,1)} %get-tuple-element.128, s32[1024]{0:T(1024)S(1)} %pad_clamp_fusion.6), kind=kCustom, calls=%fused_computation.clone.1 | custom fusion | bytes 4194432 | tf_op jit(solution)/shard_map/while/body/eval_jaxpr/gather | solution.py:35
  160.2 3.8 gather_fusion
  164.0 5.4 %gather_fusion.1 = bf16[32,512,64]{1,2,0:T(8,128)(2,1)} fusion(bf16[512,128,64]{0,2,1:T(8,128)(2,1)} %get-tuple-element.128, s32[1024]{0:T(1024)S(1)} %pad_clamp_fusion.6), kind=kCustom, calls=%fused_computation.clone.1 | custom fusion | bytes 4194432 | tf_op jit(solution)/shard_map/while/body/eval_jaxpr/gather | solution.py:35
  173.1 9.1 %gather_fusion.5 = s32[1024]{0:T(1024)S(1)} fusion(s32[4,256]{1,0:T(4,128)S(1)} %copy-done.1, s32[1024]{0:T(1024)S(1)} %bitcast.81), kind=kCustom, calls=%fused_computation.5 | custom fusion | bytes 16384 | tf_op jit(solution)/shard_map/jit(take_along_axis)/gather | solution.py:51
  182.7 143.2 %all-reduce.2.cloned.1.call-done = f32[256,4096]{1,0:T(8,128)} async-done(((f32[256,4096]{1,0:T(8,128)}), f32[256,4096]{1,0:T(8,128)}) %all-reduce.2.cloned.1.call-update) | async-done | bytes 4194320 | tf_op jit(solution)/shard_map/psum | solution.py:49
  328.2 16.0 %scatter_fusion = f32[4,16,4096]{2,1,0:T(8,128)} fusion(f32[4,16,4096]{2,1,0:T(8,128)} %broadcast_in_dim.48, s32[64]{0:T(128)S(1)} %fusion.21, f32[64,4096]{1,0:T(8,128)S(1)} %constant_dynamic-slice_fusion.2), kind=kCustom, calls=%fused_computation.6 | custom fusion | bytes 3146240 | tf_op jit(solution)/shard_map/scatter | solution.py:63
  344.2 4.2 %all-to-all-start = ((f32[4,16,4096]{2,1,0:T(8,128)}), f32[4,16,4096]{2,1,0:T(8,128)S(1)}, u32[]{:S(2)}, u32[]{:S(2)}) async-start(f32[4,16,4096]{2,1,0:T(8,128)} %scatter_fusion), calls=%async_computation | async-start | bytes 2097152 | tf_op jit(solution)/shard_map/all_to_all | solution.py:65
  348.5 13.5 %all-to-all-done = f32[4,16,4096]{2,1,0:T(8,128)S(1)} async-done(((f32[4,16,4096]{2,1,0:T(8,128)}), f32[4,16,4096]{2,1,0:T(8,128)S(1)}, u32[]{:S(2)}, u32[]{:S(2)}) %all-to-all-start) | async-done | bytes 1048608 | tf_op jit(solution)/shard_map/all_to_all | solution.py:65
  362.0 6.5 %gather_fusion.4 = f32[256,4096]{1,0:T(8,128)} fusion(f32[4,16,4096]{2,1,0:T(8,128)S(1)} %all-to-all-done, s32[256]{0:T(256)S(1)} %reshape.296), kind=kCustom, calls=%fused_computation.4 | custom fusion | bytes 8390656 | tf_op jit(solution)/shard_map/gather | solution.py:66
  (107 shorter events, 51.1 us)
Async XLA Ops:
  6.5 8.8 %copy-start = (s32[1,256]{1,0:T(1,128)S(1)}, s32[1,256]{1,0:T(1,128)}, u32[]{:S(2)}) copy-start(s32[1,256]{1,0:T(1,128)} %param.11) | copy-start | bytes 3076
  6.5 4.2 %copy-start.5 = (s32[2]{0:T(128)S(1)}, s32[2]{0:T(128)}, u32[]{:S(2)}) copy-start(s32[2]{0:T(128)} %constant.124) | copy-start | bytes 28
  6.5 4.3 %copy-start.4 = (s32[2]{0:T(128)S(1)}, s32[2]{0:T(128)}, u32[]{:S(2)}) copy-start(s32[2]{0:T(128)} %constant.127) | copy-start | bytes 28
  6.5 4.1 %copy-start.1 = (s32[4,256]{1,0:T(4,128)S(1)}, s32[4,256]{1,0:T(4,128)}, u32[]{:S(2)}) copy-start(s32[4,256]{1,0:T(4,128)} %param.14) | copy-start | bytes 12292
  6.5 4.1 %copy-start.3 = (s32[4,256]{1,0:T(4,128)S(1)}, s32[4,256]{1,0:T(4,128)}, u32[]{:S(2)}) copy-start(s32[4,256]{1,0:T(4,128)} %param.15) | copy-start | bytes 12292
  6.5 10.8 %copy-start.2 = (s32[1,256]{1,0:T(1,128)S(1)}, s32[1,256]{1,0:T(1,128)}, u32[]{:S(2)}) copy-start(s32[1,256]{1,0:T(1,128)} %param.12) | copy-start | bytes 3076
  6.6 64.0 %all-gather.2.cloned.1.call-start = ((), (), s32[]{:S(2)}) async-start(), calls=%async_computation.1 | async-start | bytes 10485760 | tf_op jit(solution)/shard_map/all_gather | solution.py:16
  10.6 315.3 %all-reduce.2.cloned.1.call-start = ((), (), s32[]{:S(2)}) async-start(), calls=%async_computation.2 | async-start | bytes 8388608 | tf_op jit(solution)/shard_map/psum | solution.py:49
  344.2 17.8 %all-to-all-start = ((f32[4,16,4096]{2,1,0:T(8,128)}), f32[4,16,4096]{2,1,0:T(8,128)S(1)}, u32[]{:S(2)}, u32[]{:S(2)}) async-start(f32[4,16,4096]{2,1,0:T(8,128)} %scatter_fusion), calls=%async_computation | async-start | bytes 2097152 | tf_op jit(solution)/shard_map/all_to_all | solution.py:65
Sparse Core Ops, SparseCore 0:
  10.7 59.8 all-gather.1
  173.2 152.6 all-reduce.1
where the time goes:
time: 384 us; the launch traced here: 379 us
  waiting for transfers between devices  197 us (51%)
  local copies, waits for them, and re-layouts  133 us (35%)
  matrix products  18.2 us (5%)
  between operations  14.3 us (4%)
  other arithmetic  11.9 us (3%)
  starting transfers between devices  4.25 us (1%)
    psum x1, waiting for transfers between devices, local(): summed = lax.psum(ordered, 'dp')  143 us
    gather x8, local copies, waits for them, and re-layouts, tile_block(): act_tiles[:, row_ids]  43.5 us
    all_gather x1, waiting for transfers between devices, local(): lax.all_gather(activations, ('tensor', 'sub'), axis=1, tiled=True)  40.2 us
    gather x8, local copies, waits for them, and re-layouts, tile_block(): cot_tiles[:, col_ids]  30.1 us
    unnamed x19, local copies, waits for them, and re-layouts  18.5 us
    dot_general x8, matrix products, tile_block(): jnp.einsum('tsa,tsb->sab', act_tiles[:, row_ids], cot_tiles[:, col_ids],...  18.2 us
    scatter x1, local copies, waits for them, and re-layouts, local(): outgoing = jnp.zeros((columns, pair_cap, BS * BS), jnp.float32).at[own_ta...  16 us
    all_to_all x1, waiting for transfers between devices, local(): lax.all_to_all(outgoing, ('tensor', 'sub'), split_axis=0, concat_axis=0,...  13.5 us
  transfers between devices with their start and end apart: 3, of which 3 were waited for; matrix products, arithmetic and copies ran while one was open for 8% of the time, Pallas kernels for 0%

commit v1 on v0

v1 whole, which is shorter than its diff:
```python
import functools

import jax
import jax.numpy as jnp
from jax import lax
from jax.experimental import pallas as pl
from jax.experimental.pallas import tpu as pltpu
from jax.sharding import PartitionSpec as P

BS = 64
HALF = 32
LANES = 128
QMAX = 32767.0
CHUNKS = 2
PIECES = 4
UNROLL = 8
MESH = pl.DeviceIdType.MESH


def kernel(
    ndp, nt, ns,
    code_ref, live_ref, src_ref, act_ref, cot_ref,
    out_ref,
    early, late, cotv, acc, sendq, sendc, recvq, recvc, total,
    cot_sem, local_sem, bsend, brecv, xsend, xrecv, fsend, frecv,
    qsend, qrecv, csend, crecv,
):
    ncol = nt * ns
    dp = lax.axis_index("dp")
    ti = lax.axis_index("tensor")
    si = lax.axis_index("sub")
    my_col = ti * ns + si
    me = dp * ncol + my_col
    owners = ndp * ncol
    feats = act_ref.shape[1]
    depth = act_ref.shape[3]
    piece = feats // PIECES
    stripes = cotv.shape[0]
    slots = acc.shape[0]
    gath = (early, late)
    pair = slots // owners

    def at(dev):
        return {"dp": dev // ncol, "tensor": lax.rem(dev, ncol) // ns, "sub": lax.rem(dev, ns)}

    def held(k, col, p=None):
        if p is None:
            return gath[k].at[pl.ds(col * feats, feats)]
        return gath[k].at[pl.ds(col * feats + p * piece, piece)]

    def stripe(i):
        return pltpu.make_async_copy(
            cot_ref.at[:, pl.ds(pl.multiple_of(i * LANES, LANES), LANES)], cotv.at[i], cot_sem.at[i]
        )

    def load(i, carry):
        stripe(i).start()
        return carry

    lax.fori_loop(0, stripes, load, 0)
    own_copies = [
        pltpu.make_async_copy(act_ref.at[k], held(k, my_col), local_sem.at[1 + k]) for k in range(CHUNKS)
    ]
    for copy in own_copies:
        copy.start()

    barrier = pltpu.get_barrier_semaphore()

    def greet(i, carry):
        dev = lax.rem(me + i, owners)
        pl.semaphore_signal(barrier, inc=1, device_id=at(dev), device_id_type=MESH)
        return carry

    lax.fori_loop(1, owners, greet, 0)
    pl.semaphore_wait(barrier, owners - 1)

    def across(o, k, p):
        return pltpu.make_async_remote_copy(
            src_ref=act_ref.at[k, pl.ds(p * piece, piece)],
            dst_ref=held(k, my_col, p),
            send_sem=xsend.at[o - 1, k, p],
            recv_sem=xrecv.at[o - 1, k, p],
            device_id={"tensor": lax.rem(ti + o, nt)},
            device_id_type=MESH,
        )

    def beside(u, k):
        return pltpu.make_async_remote_copy(
            src_ref=act_ref.at[k],
            dst_ref=held(k, my_col),
            send_sem=bsend.at[u - 1, k],
            recv_sem=brecv.at[u - 1, k],
            device_id={"sub": lax.rem(si + u, ns)},
            device_id_type=MESH,
        )

    def forward(u, o, k, p):
        col = lax.rem(ti + nt - o, nt) * ns + si
        return pltpu.make_async_remote_copy(
            src_ref=held(k, col, p),
            dst_ref=held(k, col, p),
            send_sem=fsend.at[u - 1, o - 1, k, p],
            recv_sem=frecv.at[u - 1, o - 1, k, p],
            device_id={"sub": lax.rem(si + u, ns)},
            device_id_type=MESH,
        )

    for k in range(CHUNKS):
        for p in range(PIECES):
            for o in range(1, nt):
                across(o, k, p).start()
    for k in range(CHUNKS):
        for u in range(1, ns):
            beside(u, k).start()

    def arrive(k):
        for p in range(PIECES):
            for o in range(1, nt):
                across(o, k, p).wait_recv()
                for u in range(1, ns):
                    forward(u, o, k, p).start()
        own_copies[k].wait()
        for u in range(1, ns):
            beside(u, k).wait_recv()
        for p in range(PIECES):
            for o in range(1, nt):
                for u in range(1, ns):
                    forward(u, o, k, p).wait_recv()

    def product(slot, k):
        left = gath[k][code_ref[0, slot]]
        right = cotv[code_ref[1, slot], k * depth:(k + 1) * depth, :]
        return lax.dot_general(left, right, (((1,), (0,)), ((), ())), preferred_element_type=jnp.float32)

    arrive(0)

    def loaded(i, carry):
        stripe(i).wait()
        return carry

    lax.fori_loop(0, stripes, loaded, 0)

    def first(i, carry):
        for j in range(UNROLL):
            slot = i * UNROLL + j
            value = product(slot, 0)
            acc[slot, 0] = value[:HALF]
            acc[slot, 1] = value[HALF:]
        return carry

    lax.fori_loop(0, slots // UNROLL, first, 0)
    arrive(1)

    lane = lax.broadcasted_iota(jnp.int32, (HALF, LANES), 1) // BS

    def finish(dev, j):
        slot = dev * pair + j
        odd = code_ref[2, slot]
        value = product(slot, 1)
        acc[slot, 0] += value[:HALF]
        acc[slot, 1] += value[HALF:]
        straight = acc[slot, odd]
        turned = acc[slot, code_ref[3, slot]]
        tile = jnp.where(lane == odd, straight, pltpu.roll(turned, BS, 1))
        top = jnp.maximum(jnp.max(jnp.abs(tile), axis=0, keepdims=True), 1e-30)
        coded = jnp.round(tile * (QMAX / top)).astype(jnp.int32).astype(jnp.int16)
        sendq[dev, j] = coded
        sendc[dev, j] = top * (live_ref[slot] * (1.0 / QMAX))

    def tiles_to(dev):
        return pltpu.make_async_remote_copy(
            src_ref=sendq.at[dev], dst_ref=recvq.at[me],
            send_sem=qsend.at[dev], recv_sem=qrecv.at[me],
            device_id=at(dev), device_id_type=MESH,
        )

    def scales_to(dev):
        return pltpu.make_async_remote_copy(
            src_ref=sendc.at[dev], dst_ref=recvc.at[me],
            send_sem=csend.at[dev], recv_sem=crecv.at[me],
            device_id=at(dev), device_id_type=MESH,
        )

    def tiles_from(dev):
        return pltpu.make_async_remote_copy(
            src_ref=sendq.at[dev], dst_ref=recvq.at[dev],
            send_sem=qsend.at[dev], recv_sem=qrecv.at[dev],
            device_id=at(dev), device_id_type=MESH,
        )

    def scales_from(dev):
        return pltpu.make_async_remote_copy(
            src_ref=sendc.at[dev], dst_ref=recvc.at[dev],
            send_sem=csend.at[dev], recv_sem=crecv.at[dev],
            device_id=at(dev), device_id_type=MESH,
        )

    def partner(i):
        hop = ndp - 1 - i // ncol
        col = lax.rem(my_col + ncol - 1 - lax.rem(i, ncol), ncol)
        return lax.rem(dp + hop, ndp) * ncol + col

    def second(i, carry):
        dev = partner(i)
        for j in range(pair):
            finish(dev, j)

        @pl.when(i < owners - 1)
        def _():
            tiles_to(dev).start()
            scales_to(dev).start()

        return carry

    lax.fori_loop(0, owners, second, 0)
    own_tiles = pltpu.make_async_copy(sendq.at[me], recvq.at[me], local_sem.at[0])
    own_scales = pltpu.make_async_copy(sendc.at[me], recvc.at[me], local_sem.at[1])
    own_tiles.start()
    own_scales.start()

    def collect(i, carry):
        dev = partner(i)
        tiles_from(dev).wait_recv()
        scales_from(dev).wait_recv()
        return carry

    lax.fori_loop(0, owners - 1, collect, 0)
    own_tiles.wait()
    own_scales.wait()

    here = lax.broadcasted_iota(jnp.int32, (HALF // 2, LANES), 1) < BS
    group = min(4, out_ref.shape[0])

    def settle(i, carry):
        for b in range(group):
            j = i * group + b
            col = src_ref[0, j]
            rank = src_ref[1, j]
            value = None
            for d in range(ndp):
                source = d * ncol + col
                part = recvq[source, rank].astype(jnp.int32).astype(jnp.float32)
                part = part * recvc[source, rank]
                value = part if value is None else value + part
            total[b] = value
            even = total[b, pl.ds(0, HALF // 2, stride=2), :]
            odd = total[b, pl.ds(1, HALF // 2, stride=2), :]
            out_ref[j, :HALF // 2, :] = jnp.where(here, even, pltpu.roll(odd, BS, 1))
            out_ref[j, HALF // 2:, :] = jnp.where(here, pltpu.roll(even, BS, 1), odd)
        return carry

    lax.fori_loop(0, out_ref.shape[0] // group, settle, 0)

    for k in range(CHUNKS):
        for u in range(1, ns):
            beside(u, k).wait_send()
        for p in range(PIECES):
            for o in range(1, nt):
                across(o, k, p).wait_send()
                for u in range(1, ns):
                    forward(u, o, k, p).wait_send()

    def sent(i, carry):
        dev = partner(i)
        tiles_to(dev).wait_send()
        scales_to(dev).wait_send()
        return carry

    lax.fori_loop(0, owners - 1, sent, 0)


def local(ndp, nt, ns, activations, cotangents, block_rows, block_cols, live_counts, owner_device, owner_slot):
    ncol = nt * ns
    owners = ndp * ncol
    tokens, feats = activations.shape
    slots = block_rows.shape[1]
    cap = slots // ndp
    pair = slots // owners
    depth = tokens // CHUNKS
    my_col = lax.axis_index(("tensor", "sub"))
    me = lax.axis_index("dp") * ncol + my_col

    keys = owner_device * cap + owner_slot
    key = lax.dynamic_index_in_dim(keys, my_col, 0, keepdims=False)
    position = jnp.sum((key[None, :] < key[:, None]).astype(jnp.int32), axis=1)
    match = position[None, :] == jnp.arange(slots, dtype=jnp.int32)[:, None]
    order = jnp.sum(jnp.where(match, block_rows * 1024 + block_cols, 0), axis=1)
    odd = order % 2
    codes = jnp.stack([order // 1024, order % 1024 // 2, odd, 1 - odd])
    alive = jnp.arange(slots, dtype=jnp.int32)[None, :] < live_counts[0]
    live = jnp.sum(jnp.where(match & alive, 1.0, 0.0), axis=1)

    mine = owner_device == me
    lower = owner_slot[:, None, :] < owner_slot[:, :, None]
    rank = jnp.sum((lower & mine[:, None, :]).astype(jnp.int32), axis=2)
    where_from = jnp.arange(ncol, dtype=jnp.int32)[:, None] * pair + rank
    here = mine[None] & (owner_slot[None] == jnp.arange(cap, dtype=jnp.int32)[:, None, None])
    source = jnp.sum(jnp.where(here, where_from[None], 0), axis=(1, 2))
    sources = jnp.stack([source // pair, source % pair])

    turned = activations.reshape(CHUNKS, depth, feats).transpose(0, 2, 1).reshape(CHUNKS, feats // BS, BS, depth)

    dma = pltpu.SemaphoreType.DMA
    result = pl.pallas_call(
        functools.partial(kernel, ndp, nt, ns),
        out_shape=jax.ShapeDtypeStruct((cap, HALF, LANES), jnp.float32),
        in_specs=[
            pl.BlockSpec(memory_space=pltpu.SMEM),
            pl.BlockSpec(memory_space=pltpu.SMEM),
            pl.BlockSpec(memory_space=pltpu.SMEM),
            pl.BlockSpec(memory_space=pl.ANY),
            pl.BlockSpec(memory_space=pl.ANY),
        ],
        out_specs=pl.BlockSpec(memory_space=pltpu.VMEM),
        scratch_shapes=[
            pltpu.VMEM((ncol * feats // BS, BS, depth), jnp.bfloat16),
            pltpu.VMEM((ncol * feats // BS, BS, depth), jnp.bfloat16),
            pltpu.VMEM((cotangents.shape[1] // LANES, tokens, LANES), jnp.bfloat16),
            pltpu.VMEM((slots, 2, HALF, LANES), jnp.float32),
            pltpu.VMEM((owners, pair, HALF, LANES), jnp.int16),
            pltpu.VMEM((owners, pair, 1, LANES), jnp.float32),
            pltpu.VMEM((owners, pair, HALF, LANES), jnp.int16),
            pltpu.VMEM((owners, pair, 1, LANES), jnp.float32),
            pltpu.VMEM((4, HALF, LANES), jnp.float32),
            dma((cotangents.shape[1] // LANES,)),
            dma((1 + CHUNKS,)),
            dma((ns - 1, CHUNKS)),
            dma((ns - 1, CHUNKS)),
            dma((nt - 1, CHUNKS, PIECES)),
            dma((nt - 1, CHUNKS, PIECES)),
            dma((ns - 1, nt - 1, CHUNKS, PIECES)),
            dma((ns - 1, nt - 1, CHUNKS, PIECES)),
            dma((owners,)),
            dma((owners,)),
            dma((owners,)),
            dma((owners,)),
        ],
        compiler_params=pltpu.CompilerParams(
            collective_id=0, has_side_effects=True, vmem_limit_bytes=52 * 1024 * 1024
        ),
        cost_estimate=pl.CostEstimate(flops=2 * slots * tokens * BS * LANES, bytes_accessed=16 << 20, transcendentals=0),
    )(codes, live, sources, turned, cotangents)
    return result.reshape(1, cap, BS * BS)


def solution(mesh):
    placed = (
        P(("groups", "dp"), ("tensor", "sub")),
        P(("groups", "dp"), ("tensor", "sub")),
        P(("tensor", "sub"), None),
        P(("tensor", "sub"), None),
        P(("tensor", "sub")),
        P(),
        P(),
    )
    return jax.shard_map(
        functools.partial(local, mesh.shape["dp"], mesh.shape["tensor"], mesh.shape["sub"]),
        mesh=mesh,
        in_specs=placed,
        out_specs=P(("groups", "dp", "tensor", "sub"), None, None),
        check_vma=False,
    )
```

time: 384 us -> 120 us (0.31)
  the two profiles are of different devices: /device:TPU:13 before, /device:TPU:0 now
where the time goes in v1:
time: 120 us; the launch traced here: 119 us
  Pallas kernels  109 us (91%)
  local copies, waits for them, and re-layouts  5.12 us (4%)
  other arithmetic  4.68 us (4%)
    pallas_call x1, Pallas kernels, local(): pl.pallas_call(functools.partial(kernel, ndp, nt, ns), out_shape=jax.Shap...  109 us
    reshape x1, local copies, waits for them, and re-layouts, local(): activations.reshape(CHUNKS, depth, feats).transpose(0, 2, 1)  3.96 us

profile of v1, /device:TPU:0, one launch (start us, length us, event | category | flops | bytes accessed | tf_op | source)
XLA Modules:
  0.0 119.3 jit_solution(10894027899256043251)
XLA Ops:
  0.7 0.7 broadcast_compare_fusion
  1.4 0.7 dynamic-slice_add_fusion
  2.1 0.2 convert_reduce_fusion.1
  2.3 0.1 select_reduce_fusion.1.live_ref
  2.4 0.7 multiply_add_fusion
  3.1 0.1 select_reduce_fusion.2
  3.3 1.1 convert_reduce_fusion
  4.4 0.1 broadcast_add_fusion
  4.5 0.9 select_reduce_fusion
  5.4 4.0 %copy.9 = bf16[2,256,2048]{1,2,0:T(8,128)(2,1)} copy(bf16[2,256,2048]{2,1,0:T(8,128)(2,1)} %bitcast.25) | data formatting | bytes 4194304 | tf_op jit(solution)/shard_map/reshape | solution.py:301
  9.4 108.8 %shard_map.73 = f32[64,32,128]{2,1,0:T(8,128)S(1)} custom-call(s32[4,256]{1,0:T(4,128)S(1)} %pad_add_fusion.code_ref, f32[256]{0:T(256)S(1)} %select_reduce_fusion.1.live_ref, s32[2,64]{1,0:T(2,128)S(1)} %pad_add_fusion.1.src_ref, bf16[2,32,64,256]{3,2,1,0:T(8,128)(2,1)} %bitcast.24, bf16[512,7168]{1,0:T(8,128)(2,1)} %cot_ref.1), custom_call_target="tpu_custom_call" | custom-call | flops 2147483648 | bytes 16777216 | tf_op jit(solution)/shard_map/pallas_call | solution.py:304
  118.1 1.2 reshape.271
  (7 shorter events, 0.1 us)

commit v2 on v1

--- a/solution.py
+++ b/solution.py
@@ -21,9 +21,9 @@
     ndp, nt, ns,
     code_ref, live_ref, src_ref, act_ref, cot_ref,
     out_ref,
-    early, late, cotv, acc, sendq, sendc, recvq, recvc, total,
+    early, late, cotv, acc, sendq, sendc, relayq, relayc, recvq, recvc, total,
     cot_sem, local_sem, bsend, brecv, xsend, xrecv, fsend, frecv,
-    qsend, qrecv, csend, crecv,
+    qsend, csend, rqrecv, rcrecv, qrecv, crecv,
 ):
     ncol = nt * ns
     dp = lax.axis_index("dp")
@@ -64,15 +64,31 @@
     for copy in own_copies:
         copy.start()
 
+    relayc[...] = jnp.zeros_like(relayc)
+    recvc[...] = jnp.zeros_like(recvc)
+
     barrier = pltpu.get_barrier_semaphore()
 
     def greet(i, carry):
-        dev = lax.rem(me + i, owners)
-        pl.semaphore_signal(barrier, inc=1, device_id=at(dev), device_id_type=MESH)
-        return carry
-
-    lax.fori_loop(1, owners, greet, 0)
-    pl.semaphore_wait(barrier, owners - 1)
+        z = dp + i // ncol - 1
+        dev = z * ncol + lax.rem(i, ncol)
+
+        @pl.when((z >= 0) & (z < ndp) & (dev != me))
+        def _():
+            pl.semaphore_signal(barrier, inc=1, device_id=at(dev), device_id_type=MESH)
+
+        return carry
+
+    lax.fori_loop(0, 3 * ncol, greet, 0)
+    at_end = (dp == 0) | (dp == ndp - 1)
+
+    @pl.when(at_end)
+    def _():
+        pl.semaphore_wait(barrier, 2 * ncol - 1)
+
+    @pl.when(jnp.logical_not(at_end))
+    def _():
+        pl.semaphore_wait(barrier, 3 * ncol - 1)
 
     def across(o, k, p):
         return pltpu.make_async_remote_copy(
@@ -162,69 +178,90 @@
         straight = acc[slot, odd]
         turned = acc[slot, code_ref[3, slot]]
         tile = jnp.where(lane == odd, straight, pltpu.roll(turned, BS, 1))
+        tile += relayq[dev, j].astype(jnp.int32).astype(jnp.float32) * relayc[dev, j]
         top = jnp.maximum(jnp.max(jnp.abs(tile), axis=0, keepdims=True), 1e-30)
         coded = jnp.round(tile * (QMAX / top)).astype(jnp.int32).astype(jnp.int16)
         sendq[dev, j] = coded
         sendc[dev, j] = top * (live_ref[slot] * (1.0 / QMAX))
 
-    def tiles_to(dev):
+    def send(src, dst, send_sem, recv_sem, dev):
         return pltpu.make_async_remote_copy(
-            src_ref=sendq.at[dev], dst_ref=recvq.at[me],
-            send_sem=qsend.at[dev], recv_sem=qrecv.at[me],
+            src_ref=src, dst_ref=dst, send_sem=send_sem, recv_sem=recv_sem,
             device_id=at(dev), device_id_type=MESH,
         )
 
-    def scales_to(dev):
-        return pltpu.make_async_remote_copy(
-            src_ref=sendc.at[dev], dst_ref=recvc.at[me],
-            send_sem=csend.at[dev], recv_sem=crecv.at[me],
-            device_id=at(dev), device_id_type=MESH,
-        )
-
-    def tiles_from(dev):
-        return pltpu.make_async_remote_copy(
-            src_ref=sendq.at[dev], dst_ref=recvq.at[dev],
-            send_sem=qsend.at[dev], recv_sem=qrecv.at[dev],
-            device_id=at(dev), device_id_type=MESH,
-        )
-
-    def scales_from(dev):
-        return pltpu.make_async_remote_copy(
-            src_ref=sendc.at[dev], dst_ref=recvc.at[dev],
-            send_sem=csend.at[dev], recv_sem=crecv.at[dev],
-            device_id=at(dev), device_id_type=MESH,
-        )
-
-    def partner(i):
-        hop = ndp - 1 - i // ncol
-        col = lax.rem(my_col + ncol - 1 - lax.rem(i, ncol), ncol)
-        return lax.rem(dp + hop, ndp) * ncol + col
-
-    def second(i, carry):
-        dev = partner(i)
-        for j in range(pair):
-            finish(dev, j)
-
-        @pl.when(i < owners - 1)
+    def relayed(dev, to):
+        return (
+            send(sendq.at[dev], relayq.at[dev], qsend.at[dev], rqrecv.at[dev], to),
+            send(sendc.at[dev], relayc.at[dev], csend.at[dev], rcrecv.at[dev], to),
+        )
+
+    def delivered(dev, flow, col, to):
+        return (
+            send(sendq.at[dev], recvq.at[flow, col], qsend.at[dev], qrecv.at[flow, col], to),
+            send(sendc.at[dev], recvc.at[flow, col], csend.at[dev], crecv.at[flow, col], to),
+        )
+
+    own_tiles = pltpu.make_async_copy(sendq.at[me], recvq.at[2, my_col], local_sem.at[1])
+    own_scales = pltpu.make_async_copy(sendc.at[me], recvc.at[2, my_col], local_sem.at[2])
+
+    upper = 2 * dp // ndp
+
+    def step(i, carry):
+        per = 3 * ncol
+        ring = i // per
+        col = lax.rem(my_col + 1 + lax.rem(i, ncol), ncol)
+        turn = lax.rem(i, per) // ncol
+        flow = turn + upper * (1 - 2 * turn) * (2 - turn) * (turn + 1) // 2
+        up = (1 - flow) * (2 - flow) // 2
+        down = flow * (2 - flow)
+        own = flow * (flow - 1) // 2
+        goal = up * (ndp - 1 - ring) + down * ring + own * dp
+        way = up - down
+        dev = goal * ncol + col
+        far = (goal - dp) * way
+
+        @pl.when(far + own * (1 - ring) > 0)
         def _():
-            tiles_to(dev).start()
-            scales_to(dev).start()
-
-        return carry
-
-    lax.fori_loop(0, owners, second, 0)
-    own_tiles = pltpu.make_async_copy(sendq.at[me], recvq.at[me], local_sem.at[0])
-    own_scales = pltpu.make_async_copy(sendc.at[me], recvc.at[me], local_sem.at[1])
-    own_tiles.start()
-    own_scales.start()
+            @pl.when(up * dp + down * (ndp - 1 - dp) > 0)
+            def _():
+                for copy in relayed(dev, lax.rem(me + ncol, owners)):
+                    copy.wait_recv()
+
+            for j in range(pair):
+                finish(dev, j)
+
+            @pl.when(far > 1)
+            def _():
+                for copy in relayed(dev, (dp + way) * ncol + my_col):
+                    copy.start()
+
+            @pl.when((far < 2) & (dev != me))
+            def _():
+                for copy in delivered(dev, flow, my_col, dev):
+                    copy.start()
+
+            @pl.when(dev == me)
+            def _():
+                own_tiles.start()
+                own_scales.start()
+
+        return carry
+
+    lax.fori_loop(0, (ndp - 1) * 3 * ncol, step, 0)
 
     def collect(i, carry):
-        dev = partner(i)
-        tiles_from(dev).wait_recv()
-        scales_from(dev).wait_recv()
-        return carry
-
-    lax.fori_loop(0, owners - 1, collect, 0)
+        flow = i // ncol
+        col = lax.rem(i, ncol)
+
+        @pl.when(((flow == 0) & (dp > 0)) | ((flow == 1) & (dp < ndp - 1)) | ((flow == 2) & (col != my_col)))
+        def _():
+            for copy in delivered(me, flow, col, lax.rem(me + ncol, owners)):
+                copy.wait_recv()
+
+        return carry
+
+    lax.fori_loop(0, 3 * ncol, collect, 0)
     own_tiles.wait()
     own_scales.wait()
 
@@ -237,10 +274,9 @@
             col = src_ref[0, j]
             rank = src_ref[1, j]
             value = None
-            for d in range(ndp):
-                source = d * ncol + col
-                part = recvq[source, rank].astype(jnp.int32).astype(jnp.float32)
-                part = part * recvc[source, rank]
+            for flow in range(3):
+                part = recvq[flow, col, rank].astype(jnp.int32).astype(jnp.float32)
+                part = part * recvc[flow, col, rank]
                 value = part if value is None else value + part
             total[b] = value
             even = total[b, pl.ds(0, HALF // 2, stride=2), :]
@@ -261,12 +297,12 @@
                     forward(u, o, k, p).wait_send()
 
     def sent(i, carry):
-        dev = partner(i)
-        tiles_to(dev).wait_send()
-        scales_to(dev).wait_send()
-        return carry
-
-    lax.fori_loop(0, owners - 1, sent, 0)
+        dev = lax.rem(me + i, owners)
+        for copy in relayed(dev, dev):
+            copy.wait_send()
+        return carry
+
+    lax.fori_loop(1, owners, sent, 0)
 
 
 def local(ndp, nt, ns, activations, cotangents, block_rows, block_cols, live_counts, owner_device, owner_slot):
@@ -321,6 +357,8 @@
             pltpu.VMEM((owners, pair, 1, LANES), jnp.float32),
             pltpu.VMEM((owners, pair, HALF, LANES), jnp.int16),
             pltpu.VMEM((owners, pair, 1, LANES), jnp.float32),
+            pltpu.VMEM((3, ncol, pair, HALF, LANES), jnp.int16),
+            pltpu.VMEM((3, ncol, pair, 1, LANES), jnp.float32),
             pltpu.VMEM((4, HALF, LANES), jnp.float32),
             dma((cotangents.shape[1] // LANES,)),
             dma((1 + CHUNKS,)),
@@ -334,6 +372,8 @@
             dma((owners,)),
             dma((owners,)),
             dma((owners,)),
+            dma((3, ncol)),
+            dma((3, ncol)),
         ],
         compiler_params=pltpu.CompilerParams(
             collective_id=0, has_side_effects=True, vmem_limit_bytes=52 * 1024 * 1024

time: 120 us -> 107 us (0.89)
  the two profiles are of different devices: /device:TPU:0 before, /device:TPU:13 now
where the time goes in v2:
time: 107 us
  Pallas kernels  96.6 us (90%)
  local copies, waits for them, and re-layouts  5.12 us (5%)
  other arithmetic  4.68 us (4%)
    pallas_call x1, Pallas kernels, local(): pl.pallas_call(functools.partial(kernel, ndp, nt, ns), out_shape=jax.Shap...  96.6 us
    reshape x1, local copies, waits for them, and re-layouts, local(): activations.reshape(CHUNKS, depth, feats).transpose(0, 2, 1)  3.96 us

profile of v2, /device:TPU:13, one launch (start us, length us, event | category | flops | bytes accessed | tf_op | source)
XLA Modules:
  0.0 107.1 jit_solution(13107314767719545509)
XLA Ops:
  0.7 0.7 broadcast_compare_fusion
  1.4 0.7 dynamic-slice_add_fusion
  2.1 0.2 convert_reduce_fusion.1
  2.3 0.1 select_reduce_fusion.1.live_ref
  2.4 0.7 multiply_add_fusion
  3.1 0.1 select_reduce_fusion.2
  3.3 1.1 %convert_reduce_fusion = s32[4,256]{1,0:T(4,128)S(1)} fusion(s32[4,256]{1,0:T(4,128)} %param.13, pred[4,256]{1,0:T(4,128)(4,1)S(1)} %broadcast_compare_fusion), kind=kLoop, calls=%fused_computation | loop fusion | flops 1047552 | bytes 9216 | tf_op jit(solution)/shard_map/reduce_sum | solution.py:331
  4.4 0.1 broadcast_add_fusion
  4.5 0.9 select_reduce_fusion
  5.4 4.0 %copy.9 = bf16[2,256,2048]{1,2,0:T(8,128)(2,1)} copy(bf16[2,256,2048]{2,1,0:T(8,128)(2,1)} %bitcast.25) | data formatting | bytes 4194304 | tf_op jit(solution)/shard_map/reshape | solution.py:337
  9.4 96.6 %shard_map.73 = f32[64,32,128]{2,1,0:T(8,128)S(1)} custom-call(s32[4,256]{1,0:T(4,128)S(1)} %pad_add_fusion.code_ref, f32[256]{0:T(256)S(1)} %select_reduce_fusion.1.live_ref, s32[2,64]{1,0:T(2,128)S(1)} %pad_add_fusion.1.src_ref, bf16[2,32,64,256]{3,2,1,0:T(8,128)(2,1)} %bitcast.24, bf16[512,7168]{1,0:T(8,128)(2,1)} %cot_ref.1), custom_call_target="tpu_custom_call" | custom-call | flops 2147483648 | bytes 16777216 | tf_op jit(solution)/shard_map/pallas_call | solution.py:340
  105.9 1.2 %reshape.271 = f32[1,64,4096]{2,1,0:T(8,128)} reshape(f32[64,32,128]{2,1,0:T(8,128)S(1)} %shard_map.73) | data formatting | bytes 2097152 | tf_op jit(solution)/shard_map/reshape | solution.py:383
  (7 shorter events, 0.1 us)

commit v3 on v2

--- a/solution.py
+++ b/solution.py
@@ -21,7 +21,7 @@
     ndp, nt, ns,
     code_ref, live_ref, src_ref, act_ref, cot_ref,
     out_ref,
-    early, late, cotv, acc, sendq, sendc, relayq, relayc, recvq, recvc, total,
+    actv, early, late, cotv, acc, sendq, sendc, relayq, relayc, recvq, recvc, total,
     cot_sem, local_sem, bsend, brecv, xsend, xrecv, fsend, frecv,
     qsend, csend, rqrecv, rcrecv, qrecv, crecv,
 ):
@@ -32,8 +32,8 @@
     my_col = ti * ns + si
     me = dp * ncol + my_col
     owners = ndp * ncol
-    feats = act_ref.shape[1]
-    depth = act_ref.shape[3]
+    feats = act_ref.shape[1] // BS
+    depth = act_ref.shape[0] // CHUNKS
     piece = feats // PIECES
     stripes = cotv.shape[0]
     slots = acc.shape[0]
@@ -57,12 +57,9 @@
         stripe(i).start()
         return carry
 
+    act_copy = pltpu.make_async_copy(act_ref, actv, local_sem.at[0])
+    act_copy.start()
     lax.fori_loop(0, stripes, load, 0)
-    own_copies = [
-        pltpu.make_async_copy(act_ref.at[k], held(k, my_col), local_sem.at[1 + k]) for k in range(CHUNKS)
-    ]
-    for copy in own_copies:
-        copy.start()
 
     relayc[...] = jnp.zeros_like(relayc)
     recvc[...] = jnp.zeros_like(recvc)
@@ -80,6 +77,7 @@
         return carry
 
     lax.fori_loop(0, 3 * ncol, greet, 0)
+    act_copy.wait()
     at_end = (dp == 0) | (dp == ndp - 1)
 
     @pl.when(at_end)
@@ -92,7 +90,7 @@
 
     def across(o, k, p):
         return pltpu.make_async_remote_copy(
-            src_ref=act_ref.at[k, pl.ds(p * piece, piece)],
+            src_ref=held(k, my_col, p),
             dst_ref=held(k, my_col, p),
             send_sem=xsend.at[o - 1, k, p],
             recv_sem=xrecv.at[o - 1, k, p],
@@ -102,7 +100,7 @@
 
     def beside(u, k):
         return pltpu.make_async_remote_copy(
-            src_ref=act_ref.at[k],
+            src_ref=held(k, my_col),
             dst_ref=held(k, my_col),
             send_sem=bsend.at[u - 1, k],
             recv_sem=brecv.at[u - 1, k],
@@ -123,9 +121,10 @@
 
     for k in range(CHUNKS):
         for p in range(PIECES):
+            block = actv[k * depth:(k + 1) * depth, p * piece * BS:(p + 1) * piece * BS]
+            gath[k][pl.ds(my_col * feats + p * piece, piece)] = block.T.reshape(piece, BS, depth)
             for o in range(1, nt):
                 across(o, k, p).start()
-    for k in range(CHUNKS):
         for u in range(1, ns):
             beside(u, k).start()
 
@@ -135,7 +134,6 @@
                 across(o, k, p).wait_recv()
                 for u in range(1, ns):
                     forward(u, o, k, p).start()
-        own_copies[k].wait()
         for u in range(1, ns):
             beside(u, k).wait_recv()
         for p in range(PIECES):
@@ -334,8 +332,6 @@
     source = jnp.sum(jnp.where(here, where_from[None], 0), axis=(1, 2))
     sources = jnp.stack([source // pair, source % pair])
 
-    turned = activations.reshape(CHUNKS, depth, feats).transpose(0, 2, 1).reshape(CHUNKS, feats // BS, BS, depth)
-
     dma = pltpu.SemaphoreType.DMA
     result = pl.pallas_call(
         functools.partial(kernel, ndp, nt, ns),
@@ -349,6 +345,7 @@
         ],
         out_specs=pl.BlockSpec(memory_space=pltpu.VMEM),
         scratch_shapes=[
+            pltpu.VMEM((tokens, feats), jnp.bfloat16),
             pltpu.VMEM((ncol * feats // BS, BS, depth), jnp.bfloat16),
             pltpu.VMEM((ncol * feats // BS, BS, depth), jnp.bfloat16),
             pltpu.VMEM((cotangents.shape[1] // LANES, tokens, LANES), jnp.bfloat16),
@@ -379,7 +376,7 @@
             collective_id=0, has_side_effects=True, vmem_limit_bytes=52 * 1024 * 1024
         ),
         cost_estimate=pl.CostEstimate(flops=2 * slots * tokens * BS * LANES, bytes_accessed=16 << 20, transcendentals=0),
-    )(codes, live, sources, turned, cotangents)
+    )(codes, live, sources, activations, cotangents)
     return result.reshape(1, cap, BS * BS)
 
 

time: 107 us -> 103 us (0.963)
  local copies, waits for them, and re-layouts: 5.12 us -> 1.16 us
    reshape x1 -> x0, local copies, waits for them, and re-layouts: 3.96 us -> none  [local(): activations.reshape(CHUNKS, depth, feats).transpose(0, 2, 1)]
where the time goes in v3:
time: 103 us
  Pallas kernels  96.5 us (94%)
  other arithmetic  4.68 us (5%)
  local copies, waits for them, and re-layouts  1.16 us (1%)
    pallas_call x1, Pallas kernels, local(): pl.pallas_call(functools.partial(kernel, ndp, nt, ns), out_shape=jax.Shap...  96.5 us

profile of v3, /device:TPU:13, one launch (start us, length us, event | category | flops | bytes accessed | tf_op | source)
XLA Modules:
  0.0 103.1 jit_solution(16345775657963117216)
XLA Ops:
  0.7 0.7 broadcast_compare_fusion
  1.4 0.7 dynamic-slice_add_fusion
  2.1 0.2 convert_reduce_fusion.1
  2.3 0.1 select_reduce_fusion.1.live_ref
  2.4 0.7 multiply_add_fusion
  3.1 0.1 select_reduce_fusion.2
  3.3 1.1 %convert_reduce_fusion = s32[4,256]{1,0:T(4,128)S(1)} fusion(s32[4,256]{1,0:T(4,128)} %param.13, pred[4,256]{1,0:T(4,128)(4,1)S(1)} %broadcast_compare_fusion), kind=kLoop, calls=%fused_computation | loop fusion | flops 1047552 | bytes 9216 | tf_op jit(solution)/shard_map/reduce_sum | solution.py:329
  4.4 0.1 broadcast_add_fusion
  4.5 0.9 select_reduce_fusion
  5.4 96.5 %shard_map.73 = f32[64,32,128]{2,1,0:T(8,128)S(1)} custom-call(s32[4,256]{1,0:T(4,128)S(1)} %pad_add_fusion.code_ref, f32[256]{0:T(256)S(1)} %select_reduce_fusion.1.live_ref, s32[2,64]{1,0:T(2,128)S(1)} %pad_add_fusion.1.src_ref, bf16[512,2048]{1,0:T(8,128)(2,1)} %act_ref.1, bf16[512,7168]{1,0:T(8,128)(2,1)} %cot_ref.1), custom_call_target="tpu_custom_call" | custom-call | flops 2147483648 | bytes 16777216 | tf_op jit(solution)/shard_map/pallas_call | solution.py:336
  101.9 1.2 %reshape.263 = f32[1,64,4096]{2,1,0:T(8,128)} reshape(f32[64,32,128]{2,1,0:T(8,128)S(1)} %shard_map.73) | data formatting | bytes 2097152 | tf_op jit(solution)/shard_map/reshape | solution.py:380
  (7 shorter events, 0.1 us)

commit v4 on v3

--- a/solution.py
+++ b/solution.py
@@ -19,10 +19,10 @@
 
 def kernel(
     ndp, nt, ns,
-    code_ref, live_ref, src_ref, act_ref, cot_ref,
+    rows_ref, cols_ref, live_ref, device_ref, place_ref, act_ref, cot_ref,
     out_ref,
-    actv, early, late, cotv, acc, sendq, sendc, relayq, relayc, recvq, recvc, total,
-    cot_sem, local_sem, bsend, brecv, xsend, xrecv, fsend, frecv,
+    code_rows, src_rows, code_ref, src_ref, actv, early, late, cotv, acc, sendq, sendc, relayq, relayc, recvq, recvc, total,
+    cot_sem, table_sem, local_sem, bsend, brecv, xsend, xrecv, fsend, frecv,
     qsend, csend, rqrecv, rcrecv, qrecv, crecv,
 ):
     ncol = nt * ns
@@ -146,6 +146,46 @@
         right = cotv[code_ref[1, slot], k * depth:(k + 1) * depth, :]
         return lax.dot_general(left, right, (((1,), (0,)), ((), ())), preferred_element_type=jnp.float32)
 
+    cap = out_ref.shape[0]
+    down_rows = lax.broadcasted_iota(jnp.int32, (slots, slots), 0)
+    over_lanes = lax.broadcasted_iota(jnp.int32, (slots, slots), 1)
+
+    def upright(row):
+        return jnp.sum(jnp.where(down_rows == over_lanes, row, 0), axis=1, keepdims=True)
+
+    key = device_ref[pl.ds(my_col, 1), :] * cap + place_ref[pl.ds(my_col, 1), :]
+    position = jnp.sum(jnp.where(upright(key) < key, 1, 0), axis=0, keepdims=True)
+    alive = jnp.where(over_lanes[:1] < live_ref[0], 1, 0)
+    code = upright(rows_ref[...] * 1024 + cols_ref[...] * 2 + alive)
+    order = jnp.sum(jnp.where(upright(position) == over_lanes, code, 0), axis=0, keepdims=True)
+    odd_col = (order >> 1) & 1
+    code_rows[...] = jnp.zeros_like(code_rows)
+    src_rows[...] = jnp.zeros_like(src_rows)
+    code_rows[0:1, :] = jnp.minimum(order >> 10, early.shape[0] - 1)
+    code_rows[1:2, :] = jnp.minimum((order & 1023) >> 2, stripes - 1)
+    code_rows[2:3, :] = odd_col
+    code_rows[3:4, :] = 1 - odd_col
+    code_rows[4:5, :] = order & 1
+
+    places = lax.broadcasted_iota(jnp.int32, (slots, src_rows.shape[1]), 1)
+    from_col = jnp.zeros((1, src_rows.shape[1]), jnp.int32)
+    from_rank = jnp.zeros((1, src_rows.shape[1]), jnp.int32)
+    for g in range(ncol):
+        mine = upright(jnp.where(device_ref[g:g + 1, :] == me, place_ref[g:g + 1, :], 1 << 20))
+        has = jnp.sum(jnp.where(mine == places, 1, 0), axis=0, keepdims=True)
+        from_col += has * g
+        from_rank += has * jnp.sum(jnp.where(mine < places, 1, 0), axis=0, keepdims=True)
+    src_rows[0:1, :] = jnp.minimum(from_col, ncol - 1)
+    src_rows[1:2, :] = jnp.minimum(from_rank, pair - 1)
+    tables = (
+        pltpu.make_async_copy(code_rows, code_ref, table_sem.at[0]),
+        pltpu.make_async_copy(src_rows, src_ref, table_sem.at[1]),
+    )
+    for copy in tables:
+        copy.start()
+    for copy in tables:
+        copy.wait()
+
     arrive(0)
 
     def loaded(i, carry):
@@ -180,7 +220,7 @@
         top = jnp.maximum(jnp.max(jnp.abs(tile), axis=0, keepdims=True), 1e-30)
         coded = jnp.round(tile * (QMAX / top)).astype(jnp.int32).astype(jnp.int16)
         sendq[dev, j] = coded
-        sendc[dev, j] = top * (live_ref[slot] * (1.0 / QMAX))
+        sendc[dev, j] = top * (code_ref[4, slot].astype(jnp.float32) * (1.0 / QMAX))
 
     def send(src, dst, send_sem, recv_sem, dev):
         return pltpu.make_async_remote_copy(
@@ -311,40 +351,25 @@
     cap = slots // ndp
     pair = slots // owners
     depth = tokens // CHUNKS
-    my_col = lax.axis_index(("tensor", "sub"))
-    me = lax.axis_index("dp") * ncol + my_col
-
-    keys = owner_device * cap + owner_slot
-    key = lax.dynamic_index_in_dim(keys, my_col, 0, keepdims=False)
-    position = jnp.sum((key[None, :] < key[:, None]).astype(jnp.int32), axis=1)
-    match = position[None, :] == jnp.arange(slots, dtype=jnp.int32)[:, None]
-    order = jnp.sum(jnp.where(match, block_rows * 1024 + block_cols, 0), axis=1)
-    odd = order % 2
-    codes = jnp.stack([order // 1024, order % 1024 // 2, odd, 1 - odd])
-    alive = jnp.arange(slots, dtype=jnp.int32)[None, :] < live_counts[0]
-    live = jnp.sum(jnp.where(match & alive, 1.0, 0.0), axis=1)
-
-    mine = owner_device == me
-    lower = owner_slot[:, None, :] < owner_slot[:, :, None]
-    rank = jnp.sum((lower & mine[:, None, :]).astype(jnp.int32), axis=2)
-    where_from = jnp.arange(ncol, dtype=jnp.int32)[:, None] * pair + rank
-    here = mine[None] & (owner_slot[None] == jnp.arange(cap, dtype=jnp.int32)[:, None, None])
-    source = jnp.sum(jnp.where(here, where_from[None], 0), axis=(1, 2))
-    sources = jnp.stack([source // pair, source % pair])
-
     dma = pltpu.SemaphoreType.DMA
     result = pl.pallas_call(
         functools.partial(kernel, ndp, nt, ns),
         out_shape=jax.ShapeDtypeStruct((cap, HALF, LANES), jnp.float32),
         in_specs=[
+            pl.BlockSpec(memory_space=pltpu.VMEM),
+            pl.BlockSpec(memory_space=pltpu.VMEM),
             pl.BlockSpec(memory_space=pltpu.SMEM),
-            pl.BlockSpec(memory_space=pltpu.SMEM),
-            pl.BlockSpec(memory_space=pltpu.SMEM),
+            pl.BlockSpec(memory_space=pltpu.VMEM),
+            pl.BlockSpec(memory_space=pltpu.VMEM),
             pl.BlockSpec(memory_space=pl.ANY),
             pl.BlockSpec(memory_space=pl.ANY),
         ],
         out_specs=pl.BlockSpec(memory_space=pltpu.VMEM),
         scratch_shapes=[
+            pltpu.VMEM((8, slots), jnp.int32),
+            pltpu.VMEM((8, max(cap, LANES)), jnp.int32),
+            pltpu.SMEM((8, slots), jnp.int32),
+            pltpu.SMEM((8, max(cap, LANES)), jnp.int32),
             pltpu.VMEM((tokens, feats), jnp.bfloat16),
             pltpu.VMEM((ncol * feats // BS, BS, depth), jnp.bfloat16),
             pltpu.VMEM((ncol * feats // BS, BS, depth), jnp.bfloat16),
@@ -358,6 +383,7 @@
             pltpu.VMEM((3, ncol, pair, 1, LANES), jnp.float32),
             pltpu.VMEM((4, HALF, LANES), jnp.float32),
             dma((cotangents.shape[1] // LANES,)),
+            dma((2,)),
             dma((1 + CHUNKS,)),
             dma((ns - 1, CHUNKS)),
             dma((ns - 1, CHUNKS)),
@@ -376,7 +402,7 @@
             collective_id=0, has_side_effects=True, vmem_limit_bytes=52 * 1024 * 1024
         ),
         cost_estimate=pl.CostEstimate(flops=2 * slots * tokens * BS * LANES, bytes_accessed=16 << 20, transcendentals=0),
-    )(codes, live, sources, activations, cotangents)
+    )(block_rows, block_cols, live_counts, owner_device, owner_slot, activations, cotangents)
     return result.reshape(1, cap, BS * BS)
 
 

time: 103 us -> 101 us (0.981)
  other arithmetic: 4.68 us -> 0 us
  local copies, waits for them, and re-layouts: 1.16 us -> 3.88 us
    unnamed x0 -> x8, local copies, waits for them, and re-layouts: none -> 2.72 us
    reduce_sum x5 -> x0, other arithmetic: 2.43 us -> none  [the longest x1 1.14 us: local(): rank = jnp.sum((lower & mine[:, None, :]).astype(jnp.int32), axis=2)]
    add x3 -> x0, other arithmetic: 1.48 us -> none  [the longest x1 0.71 us: local(): keys = owner_device * cap + owner_slot]
where the time goes in v4:
time: 101 us; the launch traced here: 100 us
  Pallas kernels  95.8 us (95%)
  local copies, waits for them, and re-layouts  3.88 us (4%)
    pallas_call x1, Pallas kernels, local(): pl.pallas_call(functools.partial(kernel, ndp, nt, ns), out_shape=jax.Shap...  95.8 us
    unnamed x8, local copies, waits for them, and re-layouts  2.72 us

profile of v4, /device:TPU:13, one launch (start us, length us, event | category | flops | bytes accessed | tf_op | source)
XLA Modules:
  0.0 100.3 jit_solution(15848522026988626985)
XLA Ops:
  0.7 0.0 copy-start
  0.7 0.7 copy-done
  1.3 0.0 copy-start.1
  1.3 0.7 copy-done.1
  2.0 0.0 copy-start.2
  2.0 0.7 copy-done.2
  2.7 0.0 copy-start.3
  2.7 0.7 copy-done.3
  3.4 95.8 %shard_map.73 = f32[64,32,128]{2,1,0:T(8,128)S(1)} custom-call(s32[1,256]{1,0:T(1,128)S(1)} %copy-done.2, s32[1,256]{1,0:T(1,128)S(1)} %copy-done.3, s32[1]{0:T(128)S(6)} %copy.8.live_ref, s32[4,256]{1,0:T(4,128)S(1)} %copy-done, s32[4,256]{1,0:T(4,128)S(1)} %copy-done.1, bf16[512,2048]{1,0:T(8,128)(2,1)} %act_ref.1, bf16[512,7168]{1,0:T(8,128)(2,1)} %cot_ref.1), custom_call_target="tpu_custom_call" | custom-call | flops 2147483648 | bytes 16777216 | tf_op jit(solution)/shard_map/pallas_call | solution.py:355
  99.1 1.2 %reshape.3 = f32[1,64,4096]{2,1,0:T(8,128)} reshape(f32[64,32,128]{2,1,0:T(8,128)S(1)} %shard_map.73) | data formatting | bytes 2097152 | tf_op jit(solution)/shard_map/reshape | solution.py:406
Async XLA Ops:
  0.7 0.7 copy-start
  1.3 0.7 copy-start.1
  2.0 0.7 copy-start.2
  2.7 0.7 copy-start.3
